TPU v7x, 32 devices: a whole 2x2x4 slice. The times are simulated.
32 devices in a mesh: shot: 2 (over y), freq: 4 (over z), tile: 4 (over x, core).
Axes of the slice: x: 2, y: 2, z: 4, core: 2. Of those that a mesh axis runs over, the one named last changes fastest.
Arguments:
- omega: float32 [8], P('freq'), may hold values from 30 to 150
- wavefields: float32 [4, 2, 8, 1024, 256], P('shot', None, 'freq', 'tile'), parts along dimension 0, may hold values from -2.5 to 2.5
- velocity: float32 [2, 1024, 256], P(None, ('tile', 'freq')), may hold values from 1.5 to 4.5
- eta: float32 [2, 1024, 256], P(None, ('tile', 'freq')), may hold values from 0 to 0.3
Outputs:
- image: float32 [4, 1024, 256], P('shot', ('tile', 'freq')), parts along dimension 0
There are 2 independent parts, one for each index of `shot`. A program takes and returns all parts, laid end to end along the dimension named above; an argument that names none is the same for every part. Nothing has to cross between parts.
All inputs are finite; a program needn't handle non-finite values.
Results may differ from a plain program's by a relative error of at most 0.0001.
Values sent between devices are 32-bit elements; how exact they have to be, the bound alone decides.
A program may use at most 64 MiB of HBM per device.

v0:
```python
import jax
import jax.numpy as jnp
from jax import lax
from jax.sharding import PartitionSpec as P

coeffs = ((1, 1.5), (2, -0.15), (3, 1.0 / 90.0))
centre = -49.0 / 9.0
lateral_scale = 0.5
depth_step = 0.01


def with_halo(cells, sides, width):
    for axis, dim in sides:
        count = lax.axis_size(axis)
        ends = count - 1
        head = lax.slice_in_dim(cells, 0, width, axis=dim)
        tail = lax.slice_in_dim(cells, cells.shape[dim] - width, cells.shape[dim], axis=dim)
        cells = jnp.concatenate(
            [
                lax.ppermute(tail, axis, [(i, (i + 1) % count) for i in range(ends)]),
                cells,
                lax.ppermute(head, axis, [((i + 1) % count, i) for i in range(ends)]),
            ],
            axis=dim,
        )
    return cells


def stencil(padded):
    rows = padded.shape[-2] - 6
    cols = padded.shape[-1] - 6
    core = padded[..., 3 : 3 + rows, 3 : 3 + cols]
    total = 2.0 * centre * core
    for shift, weight in coeffs:
        part = (
            padded[..., 3 + shift : 3 + shift + rows, 3 : 3 + cols]
            + padded[..., 3 - shift : 3 - shift + rows, 3 : 3 + cols]
        )
        part = (
            part
            + padded[..., 3 : 3 + rows, 3 + shift : 3 + shift + cols]
            + padded[..., 3 : 3 + rows, 3 - shift : 3 - shift + cols]
        )
        total = total + weight * part
    return total


def advance(field, lap, vel, eta_d, om):
    signs = jnp.array([-1.0, 1.0], jnp.float32).reshape((2,) + (1,) * (field.ndim - 2))
    real_part, imag_part = (field[:, 0], field[:, 1])
    lap_re, lap_im = (lap[:, 0], lap[:, 1])
    theta = lateral_scale * vel * (1.0 + 2.0 * eta_d) / om
    v_re = real_part - signs * theta * lap_im
    v_im = imag_part + signs * theta * lap_re
    phase = om * depth_step / vel
    cosine = jnp.cos(phase)
    sine = signs * jnp.sin(phase)
    out_re = cosine * v_re - sine * v_im
    out_im = cosine * v_im + sine * v_re
    term = jnp.sum(out_re[0] * out_re[1] + out_im[0] * out_im[1], axis=0)
    return (jnp.stack([out_re, out_im], axis=1), term)


def per_device(omega, wavefields, velocity, eta):
    freq_count = omega.shape[0]
    om = omega.reshape(freq_count, 1, 1)
    field = wavefields
    images = []
    for depth in range(velocity.shape[0]):
        rimmed = with_halo(field, (("tile", 3),), 3)
        padded = jnp.pad(rimmed, ((0, 0), (0, 0), (0, 0), (0, 0), (3, 3)))
        lap = stencil(padded)
        vel, eta_d = (
            lax.all_gather(velocity[depth], "freq", axis=0, tiled=True),
            lax.all_gather(eta[depth], "freq", axis=0, tiled=True),
        )
        field, term = advance(field, lap, vel, eta_d, om)
        images.append(lax.psum_scatter(term, "freq", scatter_dimension=0, tiled=True))
    return jnp.stack(images)


def solution(mesh):
    return jax.shard_map(
        per_device,
        mesh=mesh,
        in_specs=(
            P("freq"),
            P("shot", None, "freq", "tile", None),
            P(None, ("tile", "freq"), None),
            P(None, ("tile", "freq"), None),
        ),
        out_specs=P("shot", ("tile", "freq"), None),
        check_vma=False,
    )
```

profile of v0, /device:TPU:0, one launch (start us, length us, event | category | flops | bytes accessed | tf_op | source)
XLA Modules:
  0.0 145.5 jit_solution(230321352615536012)
XLA Ops:
  6.5 0.0 copy-start.2
  6.5 0.0 reduce-scatter.5.cloned.1.call-start
  6.5 0.9 fusion.46
  7.4 1.3 collective-permute-start
  8.7 3.0 %collective-permute-start.1 = (f32[2,2,2,3,256]{4,3,2,1,0:T(4,128)S(1)}, f32[2,2,2,3,256]{4,3,2,1,0:T(4,128)S(1)}, u32[]{:S(2)}, u32[]{:S(2)}) collective-permute-start(f32[2,2,2,3,256]{4,3,2,1,0:T(4,128)S(1)} %get-tuple-element.13), channel_id=1, source_target_pairs={{0,1},{1,2},{2,3},{4,5},{5,6},{6,7},{8,9},{9,10},{10,11},{12,13},{... | collective-permute-start | bytes 73736 | tf_op jit(solution)/shard_map/ppermute | solution.py:20
  11.8 0.7 broadcast_multiply_fusion
  12.4 0.9 fusion.48
  13.3 0.9 fusion.47
  14.2 16.0 %all-gather = f32[1,256,256]{2,1,0:T(8,128)S(1)} all-gather(f32[1,64,256]{2,1,0:T(8,128)S(1)} %get-tuple-element.20), channel_id=2, replica_groups=mesh['shot'=2,'freq'=4,'tile'=4] {'freq'}, dimensions={1}, use_global_device_ids=true | all-gather | bytes 327680 | tf_op jit(solution)/shard_map/all_gather | solution.py:74
  30.2 13.8 %all-gather.3 = f32[1,256,256]{2,1,0:T(8,128)S(1)} all-gather(f32[1,64,256]{2,1,0:T(8,128)S(1)} %get-tuple-element.18), channel_id=5, replica_groups=mesh['shot'=2,'freq'=4,'tile'=4] {'freq'}, dimensions={1}, use_global_device_ids=true | all-gather | bytes 327680 | tf_op jit(solution)/shard_map/all_gather | solution.py:75
  44.1 14.2 %all-gather.2 = f32[1,256,256]{2,1,0:T(8,128)S(1)} all-gather(f32[1,64,256]{2,1,0:T(8,128)S(1)} %get-tuple-element.21), channel_id=4, replica_groups=mesh['shot'=2,'freq'=4,'tile'=4] {'freq'}, dimensions={1}, use_global_device_ids=true | all-gather | bytes 327680 | tf_op jit(solution)/shard_map/all_gather | solution.py:74
  58.3 13.8 %all-gather.1 = f32[1,256,256]{2,1,0:T(8,128)S(1)} all-gather(f32[1,64,256]{2,1,0:T(8,128)S(1)} %get-tuple-element.19), channel_id=3, replica_groups=mesh['shot'=2,'freq'=4,'tile'=4] {'freq'}, dimensions={1}, use_global_device_ids=true | all-gather | bytes 327680 | tf_op jit(solution)/shard_map/all_gather | solution.py:75
  72.2 0.0 copy-done.2
  72.2 0.0 copy-start
  72.2 0.2 broadcast_divide_fusion
  72.4 3.7 %divide_cosine_fusion.1 = (f32[2,256,256]{2,1,0:T(8,128)S(1)}, f32[2,256,256]{2,1,0:T(8,128)S(1)}, f32[2,256,256]{2,1,0:T(8,128)S(1)}, f32[2,256,256]{2,1,0:T(8,128)S(1)}) fusion(f32[256,256]{1,0:T(8,128)S(1)} %bitcast.100, f32[2]{0:T(128)S(1)} %broadcast_multiply_fusion, f32[256,256]{1,0:T(8,128)S(1)} %bitcast.101), kind=kLoop, calls=%fused_computation.92 | loop fusion | flops 262144 | bytes 2621448 | tf_op jit(solution)/shard_map/cos | solution.py:56
  76.1 0.0 copy-done
  76.1 0.2 constant_dynamic-update-slice_fusion.1
  76.3 0.0 collective-permute-done
  76.4 0.0 collective-permute-done.1
  76.4 1.0 select_maximum_fusion.3
  77.4 0.0 copy-start.1
  77.4 3.0 %fusion.11 = f32[2,2,2,256,256]{4,3,2,1,0:T(8,128)S(1)} fusion(f32[2,2,2,3,256]{4,3,2,1,0:T(4,128)S(1)} %collective-permute-done.1, f32[2,2,2,262,262]{4,3,2,1,0:T(8,128)S(1)} %select_maximum_fusion.3, f32[2,2,2,256,256]{4,3,2,1,0:T(8,128)S(1)} %copy-done, f32[2,2,2,259,256]{4,3,2,1,0:T(8,128)S(1)} %constant_dynamic-update-slice_fusion), kind=kLoop, calls=%fused_computation.27 | loop fusion | flops 9961472 | bytes 23093248 | tf_op jit(solution)/shard_map/add | solution.py:44
  80.4 0.0 copy-done.1
  80.4 0.4 fusion.33
  80.8 0.4 fusion.35
  81.3 1.3 collective-permute-start.3
  82.6 1.5 %collective-permute-start.2 = (f32[2,2,2,3,256]{4,3,2,1,0:T(4,128)S(1)}, f32[2,2,2,3,256]{4,3,2,1,0:T(4,128)S(1)}, u32[]{:S(2)}, u32[]{:S(2)}) collective-permute-start(f32[2,2,2,3,256]{4,3,2,1,0:T(4,128)S(1)} %get-tuple-element.11), channel_id=1, source_target_pairs={{1,0},{2,1},{3,2},{5,4},{6,5},{7,6},{9,8},{10,9},{11,10},{13,12},{... | collective-permute-start | bytes 73736 | tf_op jit(solution)/shard_map/ppermute | solution.py:22
  84.1 0.0 collective-permute-done.3
  84.1 3.5 %collective-permute-done.2 = f32[2,2,2,3,256]{4,3,2,1,0:T(4,128)S(1)} collective-permute-done((f32[2,2,2,3,256]{4,3,2,1,0:T(4,128)S(1)}, f32[2,2,2,3,256]{4,3,2,1,0:T(4,128)S(1)}, u32[]{:S(2)}, u32[]{:S(2)}) %collective-permute-start.2) | collective-permute-done | bytes 24608 | tf_op jit(solution)/shard_map/ppermute | solution.py:22
  87.5 1.0 select_maximum_fusion
  88.6 0.4 pad_maximum_fusion.1
  89.0 2.9 %fusion.4 = f32[2,2,2,256,256]{4,3,2,1,0:T(8,128)S(1)} fusion(f32[2,1,2,256,256]{4,3,2,1,0:T(8,128)S(1)} %fusion.35, f32[2,1,2,256,256]{4,3,2,1,0:T(8,128)S(1)} %fusion.33, f32[2,2,2,262,262]{4,3,2,1,0:T(8,128)S(1)} %select_maximum_fusion, f32[2,2,2,259,256]{4,3,2,1,0:T(8,128)S(1)} %get-tuple-element.9, f32[2,2,2,259,256]{4,3,2,1,0:T(8,128)S(1)} %get-tuple-element.8), kind=kLoop, calls=%fused_computation.20 | loop fusion | flops 8912896 | bytes 29360128 | tf_op jit(solution)/shard_map/add | solution.py:44
  91.9 0.9 fusion.36
  92.8 0.6 fusion.37
  93.4 0.8 fusion.39
  94.3 0.0 reduce-scatter.5.cloned.1.call-update
  94.3 0.0 reduce-scatter.3.cloned.1.call-start
  94.4 0.8 fusion.41
  95.2 0.0 reduce-scatter.3.cloned.1.call-update
  95.2 21.6 %reduce-scatter.5.cloned.1.call-done = f32[64,256]{1,0:T(8,128)} async-done(((f32[256,256]{1,0:T(8,128)}), f32[64,256]{1,0:T(8,128)}) %reduce-scatter.5.cloned.1.call-update) | async-done | bytes 65552 | tf_op jit(solution)/shard_map/reduce_scatter | solution.py:78
  116.8 20.2 %reduce-scatter.3.cloned.1.call-done = f32[64,256]{1,0:T(8,128)} async-done(((f32[256,256]{1,0:T(8,128)}), f32[64,256]{1,0:T(8,128)}) %reduce-scatter.3.cloned.1.call-update) | async-done | bytes 65552 | tf_op jit(solution)/shard_map/reduce_scatter | solution.py:78
  137.1 1.5 %pad_maximum_fusion.3 = f32[2,64,256]{2,1,0:T(8,128)} fusion(f32[1,64,256]{2,1,0:T(8,128)} %bitcast.102, f32[1,64,256]{2,1,0:T(8,128)} %bitcast.103), kind=kLoop, calls=%fused_computation.97 | loop fusion | flops 32768 | bytes 262144 | tf_op jit(solution)/shard_map/stack | solution.py:79
  (4 shorter events, 0.1 us)
Async XLA Ops:
  6.5 65.7 %copy-start.2 = (f32[2]{0:T(128)S(1)}, f32[2]{0:T(128)}, u32[]{:S(2)}) copy-start(f32[2]{0:T(128)} %param.6) | copy-start | bytes 28
  6.5 110.3 %reduce-scatter.5.cloned.1.call-start = ((), (), s32[]{:S(2)}) async-start(), calls=%async_computation.3 | async-start | bytes 327680 | tf_op jit(solution)/shard_map/reduce_scatter | solution.py:78
  7.4 68.9 %collective-permute-start = (f32[2,2,2,3,256]{4,3,2,1,0:T(4,128)S(1)}, f32[2,2,2,3,256]{4,3,2,1,0:T(4,128)S(1)}, u32[]{:S(2)}, u32[]{:S(2)}) collective-permute-start(f32[2,2,2,3,256]{4,3,2,1,0:T(4,128)S(1)} %get-tuple-element.12), channel_id=1, source_target_pairs={{1,0},{2,1},{3,2},{5,4},{6,5},{7,6},{9,8},{10,9},{11,10},{13,12},{... | collective-permute-start | bytes 73736 | tf_op jit(solution)/shard_map/ppermute | solution.py:22
  8.7 67.6 %collective-permute-start.1 = (f32[2,2,2,3,256]{4,3,2,1,0:T(4,128)S(1)}, f32[2,2,2,3,256]{4,3,2,1,0:T(4,128)S(1)}, u32[]{:S(2)}, u32[]{:S(2)}) collective-permute-start(f32[2,2,2,3,256]{4,3,2,1,0:T(4,128)S(1)} %get-tuple-element.13), channel_id=1, source_target_pairs={{0,1},{1,2},{2,3},{4,5},{5,6},{6,7},{8,9},{9,10},{10,11},{12,13},{... | collective-permute-start | bytes 73736 | tf_op jit(solution)/shard_map/ppermute | solution.py:20
  72.2 3.9 %copy-start = (f32[2,2,2,256,256]{4,3,2,1,0:T(8,128)S(1)}, f32[2,2,2,256,256]{4,3,2,1,0:T(8,128)}, u32[]{:S(2)}) copy-start(f32[2,2,2,256,256]{4,3,2,1,0:T(8,128)} %param.7) | copy-start | bytes 6291460
  77.4 3.0 %copy-start.1 = (f32[2]{0:T(128)S(1)}, f32[2]{0:T(128)}, u32[]{:S(2)}) copy-start(f32[2]{0:T(128)} %constant.22.clone) | copy-start | bytes 28
  81.3 2.8 %collective-permute-start.3 = (f32[2,2,2,3,256]{4,3,2,1,0:T(4,128)S(1)}, f32[2,2,2,3,256]{4,3,2,1,0:T(4,128)S(1)}, u32[]{:S(2)}, u32[]{:S(2)}) collective-permute-start(f32[2,2,2,3,256]{4,3,2,1,0:T(4,128)S(1)} %get-tuple-element.10), channel_id=1, source_target_pairs={{0,1},{1,2},{2,3},{4,5},{5,6},{6,7},{8,9},{9,10},{10,11},{12,13},{... | collective-permute-start | bytes 73736 | tf_op jit(solution)/shard_map/ppermute | solution.py:20
  82.6 4.9 %collective-permute-start.2 = (f32[2,2,2,3,256]{4,3,2,1,0:T(4,128)S(1)}, f32[2,2,2,3,256]{4,3,2,1,0:T(4,128)S(1)}, u32[]{:S(2)}, u32[]{:S(2)}) collective-permute-start(f32[2,2,2,3,256]{4,3,2,1,0:T(4,128)S(1)} %get-tuple-element.11), channel_id=1, source_target_pairs={{1,0},{2,1},{3,2},{5,4},{6,5},{7,6},{9,8},{10,9},{11,10},{13,12},{... | collective-permute-start | bytes 73736 | tf_op jit(solution)/shard_map/ppermute | solution.py:22
  94.3 42.8 %reduce-scatter.3.cloned.1.call-start = ((), (), s32[]{:S(2)}) async-start(), calls=%async_computation.2 | async-start | bytes 327680 | tf_op jit(solution)/shard_map/reduce_scatter | solution.py:78
Sparse Core Ops, SparseCore 0:
  94.4 22.3 reduce-scatter.4
  119.2 17.8 reduce-scatter.2
where the time goes:
time: 146 us; the launch traced here: 145 us
  blocking collectives  57.9 us (40%)
  waiting for transfers between devices  45.4 us (31%)
  other arithmetic  18.6 us (13%)
  between operations  13.6 us (9%)
  starting transfers between devices  7.13 us (5%)
  local copies, waits for them, and re-layouts  2.91 us (2%)
    reduce_scatter x2, waiting for transfers between devices, per_device(): lax.psum_scatter(term, 'freq', scatter_dimension=0, tiled=True)  41.9 us
    all_gather x2, blocking collectives, per_device(): lax.all_gather(velocity[depth], 'freq', axis=0, tiled=True)  30.2 us
    all_gather x2, blocking collectives, per_device(): lax.all_gather(eta[depth], 'freq', axis=0, tiled=True)  27.7 us
    add x2, other arithmetic, stencil(): total = total + weight * part  5.84 us
    ppermute x2, starting transfers between devices, with_halo(): lax.ppermute(tail, axis, [(i, (i + 1) % count) for i in range(ends)])  4.32 us
    cos x1, other arithmetic, advance(): cosine = jnp.cos(phase)  3.7 us
    ppermute x2, waiting for transfers between devices, with_halo(): lax.ppermute(head, axis, [((i + 1) % count, i) for i in range(ends)])  3.46 us
  transfers between devices with their start and end apart: 6, of which 3 were waited for; matrix products, arithmetic and copies ran while one was open for 5% of the time, Pallas kernels for 0%

commit v1 on v0

--- a/solution.py
+++ b/solution.py
@@ -7,6 +7,27 @@
 centre = -49.0 / 9.0
 lateral_scale = 0.5
 depth_step = 0.01
+
+
+def laid_out(blocks, dim):
+    blocks = jnp.moveaxis(blocks, 0, dim)
+    dims = blocks.shape
+    return blocks.reshape(*dims[:dim], dims[dim] * dims[dim + 1], *dims[dim + 2 :])
+
+
+def grow_blocks(x, axis):
+    devices, mine = (lax.axis_size(axis), lax.axis_index(axis))
+    blocks, apart = (x[None], 1)
+    while apart < devices:
+        other = lax.ppermute(blocks, axis, [(i, i ^ apart) for i in range(devices)])
+        low = mine & apart == 0
+        blocks = jnp.concatenate([jnp.where(low, blocks, other), jnp.where(low, other, blocks)])
+        apart *= 2
+    return blocks
+
+
+def doubled_up(value, axis, dim):
+    return laid_out(grow_blocks(value, axis), dim)
 
 
 def with_halo(cells, sides, width):
@@ -72,7 +93,7 @@
         lap = stencil(padded)
         vel, eta_d = (
             lax.all_gather(velocity[depth], "freq", axis=0, tiled=True),
-            lax.all_gather(eta[depth], "freq", axis=0, tiled=True),
+            doubled_up(eta[depth], "freq", 0),
         )
         field, term = advance(field, lap, vel, eta_d, om)
         images.append(lax.psum_scatter(term, "freq", scatter_dimension=0, tiled=True))

time: 146 us -> 136 us (0.932)
  blocking collectives: 57.9 us -> 28.9 us
  starting transfers between devices: 7.13 us -> 13.5 us
  waiting for transfers between devices: 45.4 us -> 50.8 us
  local copies, waits for them, and re-layouts: 2.91 us -> 7.82 us
  other arithmetic: 18.6 us -> 21 us
    all_gather x2 -> x0, blocking collectives: 27.7 us -> none  [per_device(): lax.all_gather(eta[depth], 'freq', axis=0, tiled=True)]
    ppermute x0 -> x4, waiting for transfers between devices: none -> 8.25 us  [grow_blocks(): other = lax.ppermute(blocks, axis, [(i, i ^ apart) for i in range(devices)])]
    ppermute x0 -> x4, starting transfers between devices: none -> 6.58 us  [grow_blocks(): other = lax.ppermute(blocks, axis, [(i, i ^ apart) for i in range(devices)])]
    unnamed x7 -> x31, local copies, waits for them, and re-layouts: 0.23 us -> 3.81 us
    reduce_scatter x2, waiting for transfers between devices: 41.9 us -> 40 us  [per_device(): lax.psum_scatter(term, 'freq', scatter_dimension=0, tiled=True)]
  transfers between devices with their start and end apart: 6 -> 10, of which waited for: 3 -> 6; matrix products, arithmetic and copies ran while one was open for 5% -> 11% of each run, Pallas kernels for 0% -> 0%
where the time goes in v1:
time: 136 us
  waiting for transfers between devices  50.8 us (37%)
  blocking collectives  28.9 us (21%)
  other arithmetic  21 us (15%)
  between operations  13.7 us (10%)
  starting transfers between devices  13.5 us (10%)
  local copies, waits for them, and re-layouts  7.82 us (6%)
    reduce_scatter x2, waiting for transfers between devices, per_device(): lax.psum_scatter(term, 'freq', scatter_dimension=0, tiled=True)  40 us
    all_gather x2, blocking collectives, per_device(): lax.all_gather(velocity[depth], 'freq', axis=0, tiled=True)  28.9 us
    ppermute x4, waiting for transfers between devices, grow_blocks(): other = lax.ppermute(blocks, axis, [(i, i ^ apart) for i in range(devices)])  8.25 us
    ppermute x4, starting transfers between devices, grow_blocks(): other = lax.ppermute(blocks, axis, [(i, i ^ apart) for i in range(devices)])  6.58 us
    add x2, other arithmetic, stencil(): total = total + weight * part  5.82 us
    cos x1, other arithmetic, advance(): cosine = jnp.cos(phase)  4.71 us
    ppermute x2, starting transfers between devices, with_halo(): lax.ppermute(tail, axis, [(i, (i + 1) % count) for i in range(ends)])  4.32 us
    unnamed x31, local copies, waits for them, and re-layouts  3.81 us
  transfers between devices with their start and end apart: 10, of which 6 were waited for; matrix products, arithmetic and copies ran while one was open for 11% of the time, Pallas kernels for 0%

profile of v1, /device:TPU:0, one launch (start us, length us, event | category | flops | bytes accessed | tf_op | source)
XLA Modules:
  0.0 135.7 jit_solution(3476796984590326651)
XLA Ops:
  6.5 0.0 reduce-scatter.5.cloned.1.call-start
  6.5 1.6 %fusion.48 = (f32[2,2,2,3,256]{4,3,2,1,0:T(4,128)}, f32[2,2,2,3,256]{4,3,2,1,0:T(4,128)}) fusion(f32[2,2,2,256,256]{4,3,2,1,0:T(8,128)} %param.7), kind=kLoop, calls=%fused_computation.117 | loop fusion | bytes 98304 | tf_op jit(solution)/shard_map/slice | solution.py:37
  8.2 1.3 collective-permute-start.2
  9.5 3.0 %collective-permute-start.3 = (f32[2,2,2,3,256]{4,3,2,1,0:T(4,128)}, f32[2,2,2,3,256]{4,3,2,1,0:T(4,128)S(1)}, u32[]{:S(2)}, u32[]{:S(2)}) collective-permute-start(f32[2,2,2,3,256]{4,3,2,1,0:T(4,128)} %get-tuple-element.13), channel_id=1, source_target_pairs={{0,1},{1,2},{2,3},{4,5},{5,6},{6,7},{8,9},{9,10},{10,11},{12,13},{... | collective-permute-start | bytes 73736 | tf_op jit(solution)/shard_map/ppermute | solution.py:41
  12.5 0.8 slice.191
  13.4 3.0 %collective-permute-start.4 = (f32[1,64,256]{2,1,0:T(8,128)S(1)}, f32[1,64,256]{2,1,0:T(8,128)}, u32[]{:S(2)}, u32[]{:S(2)}) collective-permute-start(f32[1,64,256]{2,1,0:T(8,128)S(1)} %slice.191), channel_id=1, source_target_pairs={{0,4},{4,0},{8,12},{12,8},{1,5},{5,1},{9,13},{13,9},{2,6},{6,2},{1... | collective-permute-start | bytes 196616 | tf_op jit(solution)/shard_map/ppermute | solution.py:22
  16.4 0.7 broadcast_multiply_fusion
  17.0 0.9 fusion.49
  17.9 14.6 %all-gather = f32[1,256,256]{2,1,0:T(8,128)S(1)} all-gather(f32[1,64,256]{2,1,0:T(8,128)S(1)} %get-tuple-element.27), channel_id=2, replica_groups=mesh['shot'=2,'freq'=4,'tile'=4] {'freq'}, dimensions={1}, use_global_device_ids=true | all-gather | bytes 327680 | tf_op jit(solution)/shard_map/all_gather | solution.py:95
  32.6 14.3 %all-gather.1 = f32[1,256,256]{2,1,0:T(8,128)S(1)} all-gather(f32[1,64,256]{2,1,0:T(8,128)S(1)} %get-tuple-element.28), channel_id=3, replica_groups=mesh['shot'=2,'freq'=4,'tile'=4] {'freq'}, dimensions={1}, use_global_device_ids=true | all-gather | bytes 327680 | tf_op jit(solution)/shard_map/all_gather | solution.py:95
  46.9 0.7 copy-done.10
  47.6 4.7 %divide_cosine_fusion.1 = (f32[2,256,256]{2,1,0:T(8,128)S(1)}, f32[2,256,256]{2,1,0:T(8,128)S(1)}, f32[2,256,256]{2,1,0:T(8,128)}, f32[2,256,256]{2,1,0:T(8,128)}) fusion(f32[256,256]{1,0:T(8,128)S(1)} %bitcast.100, f32[2]{0:T(128)S(1)} %broadcast_multiply_fusion, f32[256,256]{1,0:T(8,128)S(1)} %bitcast.101), kind=kLoop, calls=%fused_computation.92 | loop fusion | flops 262144 | bytes 2621448 | tf_op jit(solution)/shard_map/cos | solution.py:77
  52.3 0.0 copy-done
  52.3 1.6 %constant_dynamic-update-slice_fusion.1 = f32[2,2,2,259,256]{4,3,2,1,0:T(8,128)} fusion(f32[2,2,2,256,256]{4,3,2,1,0:T(8,128)S(1)} %copy-done), kind=kLoop, calls=%fused_computation.115 | loop fusion | bytes 4194304
  53.9 0.0 collective-permute-done.2
  53.9 0.6 constant_dynamic-update-slice_fusion
  54.5 0.0 collective-permute-done.3
  54.5 1.0 select_maximum_fusion.3
  55.6 0.6 copy-done.1
  56.2 2.9 %fusion.11 = f32[2,2,2,256,256]{4,3,2,1,0:T(8,128)S(1)} fusion(f32[2,2,2,3,256]{4,3,2,1,0:T(4,128)S(1)} %collective-permute-done.3, f32[2,2,2,262,262]{4,3,2,1,0:T(8,128)S(1)} %select_maximum_fusion.3, f32[2,2,2,256,256]{4,3,2,1,0:T(8,128)S(1)} %copy-done, f32[2,2,2,259,256]{4,3,2,1,0:T(8,128)S(1)} %copy-done.1), kind=kLoop, calls=%fused_computation.27 | loop fusion | flops 9961472 | bytes 23093248 | tf_op jit(solution)/shard_map/add | solution.py:65
  59.1 0.0 copy-start.11
  59.1 0.0 collective-permute-done.4
  59.1 0.0 copy-done.12
  59.1 0.9 broadcast_select_fusion.5
  60.0 0.3 collective-permute-start
  60.3 0.0 copy-start.14
  60.3 2.5 %collective-permute-start.5 = (f32[2,64,256]{2,1,0:T(8,128)S(1)}, f32[2,64,256]{2,1,0:T(8,128)S(1)}, u32[]{:S(2)}, u32[]{:S(2)}) collective-permute-start(f32[2,64,256]{2,1,0:T(8,128)S(1)} %pad_maximum_fusion.4), channel_id=1, source_target_pairs={{0,8},{4,12},{8,0},{12,4},{1,9},{5,13},{9,1},{13,5},{2,10},{6,14},... | collective-permute-start | bytes 393224 | tf_op jit(solution)/shard_map/ppermute | solution.py:22
  62.8 1.9 %collective-permute-done = f32[1,64,256]{2,1,0:T(8,128)S(1)} collective-permute-done((f32[1,64,256]{2,1,0:T(8,128)S(1)}, f32[1,64,256]{2,1,0:T(8,128)S(1)}, u32[]{:S(2)}, u32[]{:S(2)}) %collective-permute-start) | collective-permute-done | bytes 65568 | tf_op jit(solution)/shard_map/ppermute | solution.py:22
  64.8 0.8 collective-permute-start.1
  65.6 2.8 %collective-permute-done.5 = f32[2,64,256]{2,1,0:T(8,128)S(1)} collective-permute-done((f32[2,64,256]{2,1,0:T(8,128)S(1)}, f32[2,64,256]{2,1,0:T(8,128)S(1)}, u32[]{:S(2)}, u32[]{:S(2)}) %collective-permute-start.5) | collective-permute-done | bytes 131104 | tf_op jit(solution)/shard_map/ppermute | solution.py:22
  68.4 0.0 copy-done.11
  68.4 0.0 copy-start.13
  68.5 3.5 %collective-permute-done.1 = f32[2,64,256]{2,1,0:T(8,128)S(1)} collective-permute-done((f32[2,64,256]{2,1,0:T(8,128)S(1)}, f32[2,64,256]{2,1,0:T(8,128)S(1)}, u32[]{:S(2)}, u32[]{:S(2)}) %collective-permute-start.1) | collective-permute-done | bytes 131104 | tf_op jit(solution)/shard_map/ppermute | solution.py:22
  72.1 0.0 copy-done.14
  72.1 0.2 broadcast_divide_fusion
  72.3 0.0 copy-done.13
  72.3 0.6 fusion.33
  73.0 0.0 copy-done.4
  73.0 0.0 copy-done.6
  73.0 0.6 fusion.35
  73.6 1.3 collective-permute-start.7
  74.9 1.3 collective-permute-start.6
  76.2 0.0 collective-permute-done.7
  76.2 2.5 %collective-permute-done.6 = f32[2,2,2,3,256]{4,3,2,1,0:T(4,128)S(1)} collective-permute-done((f32[2,2,2,3,256]{4,3,2,1,0:T(4,128)S(1)}, f32[2,2,2,3,256]{4,3,2,1,0:T(4,128)S(1)}, u32[]{:S(2)}, u32[]{:S(2)}) %collective-permute-start.6) | collective-permute-done | bytes 24608 | tf_op jit(solution)/shard_map/ppermute | solution.py:43
  78.7 1.0 select_maximum_fusion
  79.8 0.4 pad_maximum_fusion.1
  80.2 0.0 copy-start.5
  80.2 2.9 %fusion.4 = f32[2,2,2,256,256]{4,3,2,1,0:T(8,128)S(1)} fusion(f32[2,1,2,256,256]{4,3,2,1,0:T(8,128)S(1)} %fusion.35, f32[2,1,2,256,256]{4,3,2,1,0:T(8,128)S(1)} %fusion.33, f32[2,2,2,262,262]{4,3,2,1,0:T(8,128)S(1)} %select_maximum_fusion, f32[2,2,2,259,256]{4,3,2,1,0:T(8,128)S(1)} %get-tuple-element.9, f32[2,2,2,259,256]{4,3,2,1,0:T(8,128)S(1)} %get-tuple-element.8), kind=kLoop, calls=%fused_computation.20 | loop fusion | flops 8912896 | bytes 29360128 | tf_op jit(solution)/shard_map/add | solution.py:65
  83.1 0.0 copy-done.5
  83.1 0.0 copy-done.7
  83.2 0.0 copy-done.8
  83.2 0.0 copy-done.9
  83.2 1.0 fusion.36
  84.2 0.5 fusion.37
  84.7 0.5 copy-done.2
  85.2 0.8 fusion.39
  86.0 0.0 reduce-scatter.5.cloned.1.call-update
  86.0 0.0 reduce-scatter.3.cloned.1.call-start
  86.1 0.4 copy-done.3
  86.5 0.8 fusion.41
  87.3 0.0 reduce-scatter.3.cloned.1.call-update
  87.4 19.7 %reduce-scatter.5.cloned.1.call-done = f32[64,256]{1,0:T(8,128)} async-done(((f32[256,256]{1,0:T(8,128)}), f32[64,256]{1,0:T(8,128)}) %reduce-scatter.5.cloned.1.call-update) | async-done | bytes 65552 | tf_op jit(solution)/shard_map/reduce_scatter | solution.py:99
  107.1 20.3 %reduce-scatter.3.cloned.1.call-done = f32[64,256]{1,0:T(8,128)} async-done(((f32[256,256]{1,0:T(8,128)}), f32[64,256]{1,0:T(8,128)}) %reduce-scatter.3.cloned.1.call-update) | async-done | bytes 65552 | tf_op jit(solution)/shard_map/reduce_scatter | solution.py:99
  127.4 1.5 %pad_maximum_fusion.5 = f32[2,64,256]{2,1,0:T(8,128)} fusion(f32[1,64,256]{2,1,0:T(8,128)} %bitcast.102, f32[1,64,256]{2,1,0:T(8,128)} %bitcast.103), kind=kLoop, calls=%fused_computation.103 | loop fusion | flops 32768 | bytes 262144 | tf_op jit(solution)/shard_map/stack | solution.py:100
  (21 shorter events, 0.2 us)
Async XLA Ops:
  6.5 45.8 %copy-start = (f32[2,2,2,256,256]{4,3,2,1,0:T(8,128)S(1)}, f32[2,2,2,256,256]{4,3,2,1,0:T(8,128)}, u32[]{:S(2)}) copy-start(f32[2,2,2,256,256]{4,3,2,1,0:T(8,128)} %param.7) | copy-start | bytes 6291460
  6.5 100.5 %reduce-scatter.5.cloned.1.call-start = ((), (), s32[]{:S(2)}) async-start(), calls=%async_computation.3 | async-start | bytes 327680 | tf_op jit(solution)/shard_map/reduce_scatter | solution.py:99
  8.2 45.7 %collective-permute-start.2 = (f32[2,2,2,3,256]{4,3,2,1,0:T(4,128)}, f32[2,2,2,3,256]{4,3,2,1,0:T(4,128)S(1)}, u32[]{:S(2)}, u32[]{:S(2)}) collective-permute-start(f32[2,2,2,3,256]{4,3,2,1,0:T(4,128)} %get-tuple-element.12), channel_id=1, source_target_pairs={{1,0},{2,1},{3,2},{5,4},{6,5},{7,6},{9,8},{10,9},{11,10},{13,12},{... | collective-permute-start | bytes 73736 | tf_op jit(solution)/shard_map/ppermute | solution.py:43
  9.5 45.1 %collective-permute-start.3 = (f32[2,2,2,3,256]{4,3,2,1,0:T(4,128)}, f32[2,2,2,3,256]{4,3,2,1,0:T(4,128)S(1)}, u32[]{:S(2)}, u32[]{:S(2)}) collective-permute-start(f32[2,2,2,3,256]{4,3,2,1,0:T(4,128)} %get-tuple-element.13), channel_id=1, source_target_pairs={{0,1},{1,2},{2,3},{4,5},{5,6},{6,7},{8,9},{9,10},{10,11},{12,13},{... | collective-permute-start | bytes 73736 | tf_op jit(solution)/shard_map/ppermute | solution.py:41
  13.4 45.7 %collective-permute-start.4 = (f32[1,64,256]{2,1,0:T(8,128)S(1)}, f32[1,64,256]{2,1,0:T(8,128)}, u32[]{:S(2)}, u32[]{:S(2)}) collective-permute-start(f32[1,64,256]{2,1,0:T(8,128)S(1)} %slice.191), channel_id=1, source_target_pairs={{0,4},{4,0},{8,12},{12,8},{1,5},{5,1},{9,13},{13,9},{2,6},{6,2},{1... | collective-permute-start | bytes 196616 | tf_op jit(solution)/shard_map/ppermute | solution.py:22
  46.9 0.7 copy-start.10
  52.3 20.7 %copy-start.4 = (f32[2,256,256]{2,1,0:T(8,128)}, f32[2,256,256]{2,1,0:T(8,128)S(1)}, u32[]{:S(2)}) copy-start(f32[2,256,256]{2,1,0:T(8,128)S(1)} %get-tuple-element.14) | copy-start | bytes 1572868
  52.3 20.7 %copy-start.6 = (f32[2,256,256]{2,1,0:T(8,128)}, f32[2,256,256]{2,1,0:T(8,128)S(1)}, u32[]{:S(2)}) copy-start(f32[2,256,256]{2,1,0:T(8,128)S(1)} %get-tuple-element.15) | copy-start | bytes 1572868
  54.5 1.6 %copy-start.1 = (f32[2,2,2,259,256]{4,3,2,1,0:T(8,128)S(1)}, f32[2,2,2,259,256]{4,3,2,1,0:T(8,128)}, u32[]{:S(2)}) copy-start(f32[2,2,2,259,256]{4,3,2,1,0:T(8,128)} %constant_dynamic-update-slice_fusion) | copy-start | bytes 6365188
  56.2 3.0 %copy-start.12 = (f32[2,64,256]{2,1,0:T(8,128)S(1)}, f32[2,64,256]{2,1,0:T(8,128)}, u32[]{:S(2)}) copy-start(f32[2,64,256]{2,1,0:T(8,128)} %param.9) | copy-start | bytes 393220
  59.1 9.3 %copy-start.11 = (f32[1,256,256]{2,1,0:T(8,128)S(1)}, f32[1,256,256]{2,1,0:T(8,128)}, u32[]{:S(2)}) copy-start(f32[1,256,256]{2,1,0:T(8,128)} %copy-done.10) | copy-start | bytes 786436
  60.0 4.7 %collective-permute-start = (f32[1,64,256]{2,1,0:T(8,128)S(1)}, f32[1,64,256]{2,1,0:T(8,128)S(1)}, u32[]{:S(2)}, u32[]{:S(2)}) collective-permute-start(f32[1,64,256]{2,1,0:T(8,128)S(1)} %get-tuple-element.26), channel_id=1, source_target_pairs={{0,4},{4,0},{8,12},{12,8},{1,5},{5,1},{9,13},{13,9},{2,6},{6,2},{1... | collective-permute-start | bytes 196616 | tf_op jit(solution)/shard_map/ppermute | solution.py:22
  60.3 11.8 %copy-start.14 = (f32[2]{0:T(128)S(1)}, f32[2]{0:T(128)}, u32[]{:S(2)}) copy-start(f32[2]{0:T(128)} %param.6) | copy-start | bytes 28
  60.3 8.1 %collective-permute-start.5 = (f32[2,64,256]{2,1,0:T(8,128)S(1)}, f32[2,64,256]{2,1,0:T(8,128)S(1)}, u32[]{:S(2)}, u32[]{:S(2)}) collective-permute-start(f32[2,64,256]{2,1,0:T(8,128)S(1)} %pad_maximum_fusion.4), channel_id=1, source_target_pairs={{0,8},{4,12},{8,0},{12,4},{1,9},{5,13},{9,1},{13,5},{2,10},{6,14},... | collective-permute-start | bytes 393224 | tf_op jit(solution)/shard_map/ppermute | solution.py:22
  64.8 7.2 %collective-permute-start.1 = (f32[2,64,256]{2,1,0:T(8,128)S(1)}, f32[2,64,256]{2,1,0:T(8,128)S(1)}, u32[]{:S(2)}, u32[]{:S(2)}) collective-permute-start(f32[2,64,256]{2,1,0:T(8,128)S(1)} %pad_maximum_fusion.3), channel_id=1, source_target_pairs={{0,8},{4,12},{8,0},{12,4},{1,9},{5,13},{9,1},{13,5},{2,10},{6,14},... | collective-permute-start | bytes 393224 | tf_op jit(solution)/shard_map/ppermute | solution.py:22
  68.4 3.9 %copy-start.13 = (f32[2]{0:T(128)S(1)}, f32[2]{0:T(128)}, u32[]{:S(2)}) copy-start(f32[2]{0:T(128)} %constant.32.clone) | copy-start | bytes 28
  73.6 2.6 %collective-permute-start.7 = (f32[2,2,2,3,256]{4,3,2,1,0:T(4,128)S(1)}, f32[2,2,2,3,256]{4,3,2,1,0:T(4,128)S(1)}, u32[]{:S(2)}, u32[]{:S(2)}) collective-permute-start(f32[2,2,2,3,256]{4,3,2,1,0:T(4,128)S(1)} %get-tuple-element.10), channel_id=1, source_target_pairs={{0,1},{1,2},{2,3},{4,5},{5,6},{6,7},{8,9},{9,10},{10,11},{12,13},{... | collective-permute-start | bytes 73736 | tf_op jit(solution)/shard_map/ppermute | solution.py:41
  74.9 3.8 %collective-permute-start.6 = (f32[2,2,2,3,256]{4,3,2,1,0:T(4,128)S(1)}, f32[2,2,2,3,256]{4,3,2,1,0:T(4,128)S(1)}, u32[]{:S(2)}, u32[]{:S(2)}) collective-permute-start(f32[2,2,2,3,256]{4,3,2,1,0:T(4,128)S(1)} %get-tuple-element.11), channel_id=1, source_target_pairs={{1,0},{2,1},{3,2},{5,4},{6,5},{7,6},{9,8},{10,9},{11,10},{13,12},{... | collective-permute-start | bytes 73736 | tf_op jit(solution)/shard_map/ppermute | solution.py:43
  80.2 2.9 %copy-start.5 = (f32[2,256,256]{2,1,0:T(8,128)S(1)}, f32[2,256,256]{2,1,0:T(8,128)}, u32[]{:S(2)}) copy-start(f32[2,256,256]{2,1,0:T(8,128)} %copy-done.4) | copy-start | bytes 1572868
  80.2 2.9 %copy-start.7 = (f32[2,256,256]{2,1,0:T(8,128)S(1)}, f32[2,256,256]{2,1,0:T(8,128)}, u32[]{:S(2)}) copy-start(f32[2,256,256]{2,1,0:T(8,128)} %copy-done.6) | copy-start | bytes 1572868
  80.2 2.9 %copy-start.8 = (f32[2,256,256]{2,1,0:T(8,128)S(1)}, f32[2,256,256]{2,1,0:T(8,128)}, u32[]{:S(2)}) copy-start(f32[2,256,256]{2,1,0:T(8,128)} %get-tuple-element.31) | copy-start | bytes 1572868
  80.2 2.9 %copy-start.9 = (f32[2,256,256]{2,1,0:T(8,128)S(1)}, f32[2,256,256]{2,1,0:T(8,128)}, u32[]{:S(2)}) copy-start(f32[2,256,256]{2,1,0:T(8,128)} %get-tuple-element.32) | copy-start | bytes 1572868
  84.2 1.0 copy-start.2
  85.2 1.3 copy-start.3
  86.0 41.3 %reduce-scatter.3.cloned.1.call-start = ((), (), s32[]{:S(2)}) async-start(), calls=%async_computation.2 | async-start | bytes 327680 | tf_op jit(solution)/shard_map/reduce_scatter | solution.py:99
Sparse Core Ops, SparseCore 0:
  86.1 20.8 reduce-scatter.4
  109.4 17.8 reduce-scatter.2
